TPU v7x, 32 devices: a whole 2x2x4 slice. The times are simulated.
32 devices in a mesh: ctx: 16 (over z, y, core), chan: 2 (over x).
Axes of the slice: x: 2, y: 2, z: 4, core: 2. Of those that a mesh axis runs over, the one named last changes fastest.
Arguments:
- sequence: bfloat16 [2048, 4096], P('ctx', 'chan'), may hold values from -6 to 6
- in_weight: bfloat16 [3, 4096, 2048], P(None, 'ctx', 'chan'), may hold values from -0.09375 to 0.09375
- short_taps: float32 [3, 7, 2048], P(None, None, 'chan'), may hold values from -2 to 2
- decay_rates: float32 [128, 16], P('chan'), may hold values from 0.00012207031 to 0.03
- residues: float32 [128, 16], P('chan'), may hold values from -1.5 to 1.5
- skip_gain: float32 [2048], P('chan'), may hold values from -5 to 5
Outputs:
- mixed: bfloat16 [2048, 2048], P('ctx', 'chan')
All inputs are finite; a program needn't handle non-finite values.
Results may differ from a plain program's by a relative error of at most 0.0064.
Values may be sent and summed in bfloat16 or wider, within the bound.
A program may use at most 64 MiB of HBM per device.

v0:
```python
import math

import jax
import jax.numpy as jnp
from jax import lax
from jax.sharding import PartitionSpec as P

FGROUP = 16


HIGHEST = lax.Precision.HIGHEST


def shifted(block, axis, distance):
    devices = range(lax.axis_size(axis))
    route = [(i - distance, i) for i in devices if i - distance in devices]
    return lax.ppermute(block, axis, route)


def rotation(numerator, period):
    angle = -2.0 * math.pi / period * numerator.astype(jnp.float32)
    return (jnp.cos(angle), jnp.sin(angle))


def complex_times(real_part, imag_part, cosine, sine):
    return (real_part * cosine - imag_part * sine, real_part * sine + imag_part * cosine)


def rotate_field(field, cosine, sine):
    real_part, imag_part = complex_times(field[0], field[1], cosine, sine)
    return jnp.stack([real_part, imag_part])


def open_padding(real_part, imag_part, offsets, fft_length):
    cosine, sine = rotation(offsets, fft_length)
    turned_real, turned_imag = complex_times(real_part, imag_part, cosine[:, None], sine[:, None])
    return jnp.stack([jnp.stack([real_part, turned_real]), jnp.stack([imag_part, turned_imag])])


def close_padding(field, offsets, fft_length):
    cosine, sine = rotation(offsets, fft_length)
    turned_real, turned_imag = complex_times(
        field[0, 1], field[1, 1], cosine[:, None], -sine[:, None]
    )
    return ((field[0, 0] + turned_real) / fft_length, (field[1, 0] + turned_imag) / fft_length)


def dft_table(length, sign):
    indices = jnp.arange(length, dtype=jnp.int32)
    products = indices[:, None] * indices[None, :] % length
    angle = sign * 2.0 * math.pi / length * products.astype(jnp.float32)
    return (jnp.cos(angle), jnp.sin(angle))


def apply_table(table, field):
    cosine, sine = table
    real_out = jnp.einsum("kp,hpqw->hkqw", cosine, field[0], precision=HIGHEST) - jnp.einsum(
        "kp,hpqw->hkqw", sine, field[1], precision=HIGHEST
    )
    imag_out = jnp.einsum("kp,hpqw->hkqw", cosine, field[1], precision=HIGHEST) + jnp.einsum(
        "kp,hpqw->hkqw", sine, field[0], precision=HIGHEST
    )
    return jnp.stack([real_out, imag_out])


def middle_rotation(field, device_pos, count, quarter, seq_length, sign):
    columns = device_pos * quarter + jnp.arange(quarter, dtype=jnp.int32)
    cosine, sine = rotation(
        jnp.arange(count, dtype=jnp.int32)[:, None] * columns[None, :] % seq_length, seq_length
    )
    return rotate_field(field, cosine[:, :, None], sign * sine[:, :, None])


def apply_response(spectrum, response, group_pairs):
    shape = spectrum.shape
    grouped = spectrum.reshape(shape[0], shape[1], shape[2], response.shape[3], group_pairs)
    real_part, imag_part = complex_times(
        grouped[0], grouped[1], response[0][..., None], response[1][..., None]
    )
    return jnp.stack([real_part, imag_part]).reshape(shape)


def per_device(sequence, in_weight, short_taps, decay_rates, residues, skip_gain):
    whole = lax.all_gather(sequence, "chan", axis=1, tiled=True)
    row_count = whole.shape[0]
    lane_count = in_weight.shape[2]
    projections = jnp.einsum(
        "td,sdc->stc",
        whole,
        lax.all_gather(in_weight, "ctx", axis=1, tiled=True),
        preferred_element_type=jnp.float32,
    ).astype(jnp.bfloat16)
    tap_count = short_taps.shape[1]
    edge = shifted(projections[:, row_count - (tap_count - 1) :, :], "ctx", 1)
    extended = jnp.concatenate([edge, projections], axis=1)
    filtered = jnp.zeros((3, row_count, lane_count), jnp.float32)
    for tap_index in range(tap_count):
        begin = tap_count - 1 - tap_index
        filtered = filtered + short_taps[:, tap_index, None, :] * extended[
            :, begin : begin + row_count, :
        ].astype(jnp.float32)
    query = filtered[0]
    signal = filtered[1] * filtered[2]
    device_pos = lax.axis_index("ctx")
    count = lax.axis_size("ctx")
    seq_length = row_count * count
    fft_length = 2 * seq_length
    offsets = device_pos * row_count + jnp.arange(row_count, dtype=jnp.int32)
    moments = offsets.astype(jnp.float32)
    mode_weights = residues * jnp.sqrt(2.0 * decay_rates)
    impulse = jnp.sum(
        mode_weights[None, :, :] * jnp.exp(-decay_rates[None, :, :] * moments[:, None, None]),
        axis=2,
    )
    paired = signal.reshape(row_count, lane_count // 2, 2)
    spectrum = open_padding(paired[:, :, 0], paired[:, :, 1], offsets, fft_length)
    response = open_padding(impulse, jnp.zeros_like(impulse), offsets, fft_length)
    quarter = row_count // count
    across_forward = dft_table(count, -1.0)
    within_forward = dft_table(row_count, -1.0)
    across_back = dft_table(count, 1.0)
    within_back = dft_table(row_count, 1.0)
    moved_signal, moved_response = (
        lax.all_to_all(spectrum[:, :, None], "ctx", split_axis=3, concat_axis=2, tiled=True),
        lax.all_to_all(response[:, :, None], "ctx", split_axis=3, concat_axis=2, tiled=True),
    )
    moved_signal = middle_rotation(
        apply_table(across_forward, moved_signal), device_pos, count, quarter, seq_length, 1.0
    )
    moved_response = middle_rotation(
        apply_table(across_forward, moved_response), device_pos, count, quarter, seq_length, 1.0
    )
    spread_signal, spread_response = (
        lax.all_to_all(moved_signal, "ctx", split_axis=2, concat_axis=3, tiled=True),
        lax.all_to_all(moved_response, "ctx", split_axis=2, concat_axis=3, tiled=True),
    )
    spectrum = apply_table(within_forward, spread_signal[:, :, 0][:, :, :, None])[:, :, :, 0]
    response = apply_table(within_forward, spread_response[:, :, 0][:, :, :, None])[:, :, :, 0]
    product = apply_response(spectrum, response, FGROUP // 2)
    returned = apply_table(within_back, product[:, :, :, None])[:, :, :, 0]
    returned = lax.all_to_all(returned[:, :, None], "ctx", split_axis=3, concat_axis=2, tiled=True)
    returned = apply_table(
        across_back, middle_rotation(returned, device_pos, count, quarter, seq_length, -1.0)
    )
    returned = lax.all_to_all(returned, "ctx", split_axis=2, concat_axis=3, tiled=True)
    product = returned[:, :, 0]
    conv_real, conv_imag = close_padding(product, offsets, fft_length)
    conv = jnp.stack([conv_real, conv_imag], axis=2).reshape(row_count, lane_count)
    return (query * (conv + skip_gain * signal)).astype(jnp.bfloat16)


def solution(mesh):
    return jax.shard_map(
        per_device,
        mesh=mesh,
        in_specs=(
            P("ctx", "chan"),
            P(None, "ctx", "chan"),
            P(None, None, "chan"),
            P("chan", None),
            P("chan", None),
            P("chan"),
        ),
        out_specs=P("ctx", "chan"),
        check_vma=False,
    )
```

profile of v0, /device:TPU:0, one launch (start us, length us, event | category | flops | bytes accessed | tf_op | source)
XLA Modules:
  0.0 340.0 jit_solution(2820850543408848044)
XLA Ops:
  9.9 7.4 %all-to-all-start.2 = ((f32[16,1,2048]{2,1,0:T(1,128)}), f32[16,1,2048]{2,1,0:T(1,128)S(1)}, u32[]{:S(2)}, u32[]{:S(2)}) async-start(f32[16,1,2048]{2,1,0:T(1,128)} %reshape.634), calls=%async_computation.2 | async-start | bytes 262144 | tf_op jit(solution)/shard_map/all_to_all | solution.py:125
  17.4 15.6 %all-gather.5.cloned.1.call-done = bf16[128,4096]{1,0:T(8,128)(2,1)} async-done(((bf16[128,2048]{1,0:T(8,128)(2,1)}), bf16[128,4096]{1,0:T(8,128)(2,1)}) %all-gather.5.cloned.1.call-update) | async-done | bytes 1048592 | tf_op jit(solution)/shard_map/all_gather | solution.py:84
  32.9 130.1 %all-gather.3.cloned.1.call-done = bf16[3,4096,1024]{2,1,0:T(8,128)(2,1)} async-done(((bf16[3,256,1024]{2,1,0:T(8,128)(2,1)}), bf16[3,4096,1024]{2,1,0:T(8,128)(2,1)}) %all-gather.3.cloned.1.call-update) | async-done | bytes 25165840 | tf_op jit(solution)/shard_map/all_gather | solution.py:90
  163.1 11.9 %fusion = bf16[3,128,1024]{2,1,0:T(8,128)(2,1)S(1)} fusion(bf16[3,4096,1024]{2,1,0:T(8,128)(2,1)} %all-gather.3.cloned.1.call-done, bf16[128,4096]{1,0:T(8,128)(2,1)} %all-gather.5.cloned.1.call-done), kind=kOutput, calls=%fused_computation.7 | convolution fusion | flops 3221618688 | bytes 27000832 | tf_op jit(solution)/shard_map/td,sdc->stc/dot_general | solution.py:87
  175.0 2.2 collective-permute-start
  178.1 1.5 multiply_add_fusion
  180.7 1.3 copy.104
  182.1 8.0 %all-to-all-start = ((f32[2,2,1,128,512]{4,1,0,2,3:T(2,128)}), f32[2,2,1,128,512]{4,1,0,2,3:T(2,128)S(1)}, u32[]{:S(2)}, u32[]{:S(2)}) async-start(f32[2,2,1,128,512]{4,1,0,2,3:T(2,128)} %copy.104), calls=%async_computation | async-start | bytes 2097152 | tf_op jit(solution)/shard_map/all_to_all | solution.py:124
  194.3 18.7 %all-to-all-done = f32[2,2,1,128,512]{4,1,0,2,3:T(2,128)S(1)} async-done(((f32[2,2,1,128,512]{4,1,0,2,3:T(2,128)}), f32[2,2,1,128,512]{4,1,0,2,3:T(2,128)S(1)}, u32[]{:S(2)}, u32[]{:S(2)}) %all-to-all-start) | async-done | bytes 1048608 | tf_op jit(solution)/shard_map/all_to_all | solution.py:124
  213.0 6.9 %all-to-all-start.3 = ((f32[16,1,2048]{2,1,0:T(1,128)}), f32[16,1,2048]{2,1,0:T(1,128)S(1)}, u32[]{:S(2)}, u32[]{:S(2)}) async-start(f32[16,1,2048]{2,1,0:T(1,128)} %reshape.636), calls=%async_computation.3 | async-start | bytes 262144 | tf_op jit(solution)/shard_map/all_to_all | solution.py:135
  224.4 1.6 copy.111
  226.0 1.8 all-to-all-done.3
  227.8 4.2 %all-to-all-start.1 = ((f32[2,2,16,8,512]{4,3,1,0,2:T(8,128)}), f32[2,2,16,8,512]{4,3,1,0,2:T(8,128)S(1)}, u32[]{:S(2)}, u32[]{:S(2)}) async-start(f32[2,2,16,8,512]{4,3,1,0,2:T(8,128)} %copy.111), calls=%async_computation.1 | async-start | bytes 2097152 | tf_op jit(solution)/shard_map/all_to_all | solution.py:134
  235.1 19.9 %all-to-all-done.1 = f32[2,2,16,8,512]{4,3,1,0,2:T(8,128)S(1)} async-done(((f32[2,2,16,8,512]{4,3,1,0,2:T(8,128)}), f32[2,2,16,8,512]{4,3,1,0,2:T(8,128)S(1)}, u32[]{:S(2)}, u32[]{:S(2)}) %all-to-all-start.1) | async-done | bytes 1048608 | tf_op jit(solution)/shard_map/all_to_all | solution.py:134
  258.4 1.1 fusion.6
  263.0 1.3 copy.134
  264.3 31.7 %all_to_all.24 = f32[2,2,1,128,512]{4,1,0,2,3:T(2,128)S(1)} all-to-all(f32[2,2,1,128,512]{4,1,0,2,3:T(2,128)} %copy.134), channel_id=1, replica_groups=mesh['ctx'=16,'chan'=2] {'ctx'}, dimensions={3} | all-to-all | bytes 2097152 | tf_op jit(solution)/shard_map/all_to_all | solution.py:141
  296.6 1.3 fusion.61
  297.9 1.3 fusion.60
  299.1 1.3 fusion.1
  300.4 1.3 fusion.2
  301.9 1.6 copy.141
  303.5 5.0 %all-to-all-start.5 = ((f32[2,2,16,8,512]{4,3,1,0,2:T(8,128)}), f32[2,2,16,8,512]{4,3,1,0,2:T(8,128)S(1)}, u32[]{:S(2)}, u32[]{:S(2)}) async-start(f32[2,2,16,8,512]{4,3,1,0,2:T(8,128)} %copy.141), calls=%async_computation.5 | async-start | bytes 2097152 | tf_op jit(solution)/shard_map/all_to_all | solution.py:145
  308.5 22.9 %all-to-all-done.5 = f32[2,2,16,8,512]{4,3,1,0,2:T(8,128)S(1)} async-done(((f32[2,2,16,8,512]{4,3,1,0,2:T(8,128)}), f32[2,2,16,8,512]{4,3,1,0,2:T(8,128)S(1)}, u32[]{:S(2)}, u32[]{:S(2)}) %all-to-all-start.5) | async-done | bytes 1048608 | tf_op jit(solution)/shard_map/all_to_all | solution.py:145
  (92 shorter events, 26.2 us)
Async XLA Ops:
  6.5 1.5 copy-start.1
  6.5 1.5 copy-start.2
  6.5 26.4 %all-gather.5.cloned.1.call-start = ((), (), s32[]{:S(2)}) async-start(), calls=%async_computation.7 | async-start | bytes 1572864 | tf_op jit(solution)/shard_map/all_gather | solution.py:84
  7.3 10.0 %copy-start = (f32[3,7,1024]{2,1,0:T(8,128)S(1)}, f32[3,7,1024]{2,1,0:T(8,128)}, u32[]{:S(2)}) copy-start(f32[3,7,1024]{2,1,0:T(8,128)} %param.8) | copy-start | bytes 258052
  7.3 155.8 %all-gather.3.cloned.1.call-start = ((), (), s32[]{:S(2)}) async-start(), calls=%async_computation.6 | async-start | bytes 26738688 | tf_op jit(solution)/shard_map/all_gather | solution.py:90
  9.9 172.2 %all-to-all-start.2 = ((f32[16,1,2048]{2,1,0:T(1,128)}), f32[16,1,2048]{2,1,0:T(1,128)S(1)}, u32[]{:S(2)}, u32[]{:S(2)}) async-start(f32[16,1,2048]{2,1,0:T(1,128)} %reshape.634), calls=%async_computation.2 | async-start | bytes 262144 | tf_op jit(solution)/shard_map/all_to_all | solution.py:125
  175.0 3.0 collective-permute-start
  182.1 30.9 %all-to-all-start = ((f32[2,2,1,128,512]{4,1,0,2,3:T(2,128)}), f32[2,2,1,128,512]{4,1,0,2,3:T(2,128)S(1)}, u32[]{:S(2)}, u32[]{:S(2)}) async-start(f32[2,2,1,128,512]{4,1,0,2,3:T(2,128)} %copy.104), calls=%async_computation | async-start | bytes 2097152 | tf_op jit(solution)/shard_map/all_to_all | solution.py:124
  213.0 14.8 %all-to-all-start.3 = ((f32[16,1,2048]{2,1,0:T(1,128)}), f32[16,1,2048]{2,1,0:T(1,128)S(1)}, u32[]{:S(2)}, u32[]{:S(2)}) async-start(f32[16,1,2048]{2,1,0:T(1,128)} %reshape.636), calls=%async_computation.3 | async-start | bytes 262144 | tf_op jit(solution)/shard_map/all_to_all | solution.py:135
  227.8 27.2 %all-to-all-start.1 = ((f32[2,2,16,8,512]{4,3,1,0,2:T(8,128)}), f32[2,2,16,8,512]{4,3,1,0,2:T(8,128)S(1)}, u32[]{:S(2)}, u32[]{:S(2)}) async-start(f32[2,2,16,8,512]{4,3,1,0,2:T(8,128)} %copy.111), calls=%async_computation.1 | async-start | bytes 2097152 | tf_op jit(solution)/shard_map/all_to_all | solution.py:134
  303.5 27.9 %all-to-all-start.5 = ((f32[2,2,16,8,512]{4,3,1,0,2:T(8,128)}), f32[2,2,16,8,512]{4,3,1,0,2:T(8,128)S(1)}, u32[]{:S(2)}, u32[]{:S(2)}) async-start(f32[2,2,16,8,512]{4,3,1,0,2:T(8,128)} %copy.141), calls=%async_computation.5 | async-start | bytes 2097152 | tf_op jit(solution)/shard_map/all_to_all | solution.py:145
  331.6 0.7 copy-start.3
Sparse Core Ops, SparseCore 0:
  8.9 23.9 all-gather.4
  34.5 128.5 all-gather.2
where the time goes:
time: 342 us; the launch traced here: 340 us
  waiting for transfers between devices  211 us (62%)
  starting transfers between devices  33.6 us (10%)
  matrix products  31.9 us (9%)
  blocking collectives  31.7 us (9%)
  between operations  14 us (4%)
  local copies, waits for them, and re-layouts  11.9 us (3%)
  other arithmetic  5.6 us (2%)
    all_gather x1, waiting for transfers between devices, per_device(): lax.all_gather(in_weight, 'ctx', axis=1, tiled=True)  130 us
    all_to_all x1, blocking collectives, per_device(): lax.all_to_all(returned[:, :, None], 'ctx', split_axis=3, concat_axis=2,...  31.7 us
    all_to_all x1, waiting for transfers between devices, per_device(): lax.all_to_all(returned, 'ctx', split_axis=2, concat_axis=3, tiled=True)  22.9 us
    all_to_all x1, waiting for transfers between devices, per_device(): lax.all_to_all(moved_signal, 'ctx', split_axis=2, concat_axis=3, tiled=True)  19.9 us
    all_to_all x1, waiting for transfers between devices, per_device(): lax.all_to_all(spectrum[:, :, None], 'ctx', split_axis=3, concat_axis=2,...  18.7 us
    all_gather x1, waiting for transfers between devices, per_device(): whole = lax.all_gather(sequence, 'chan', axis=1, tiled=True)  15.6 us
    dot_general x1, matrix products, per_device(): jnp.einsum('td,sdc->stc', whole, lax.all_gather(in_weight, 'ctx', axis=1,...  11.9 us
    all_to_all x1, starting transfers between devices, per_device(): lax.all_to_all(spectrum[:, :, None], 'ctx', split_axis=3, concat_axis=2,...  7.98 us
  transfers between devices with their start and end apart: 8, of which 7 were waited for; matrix products, arithmetic and copies ran while one was open for 9% of the time, Pallas kernels for 0%

commit v1 on v0

--- a/solution.py
+++ b/solution.py
@@ -1,11 +1,15 @@
+import functools
 import math
 
 import jax
 import jax.numpy as jnp
 from jax import lax
+from jax.experimental import pallas as pl
+from jax.experimental.pallas import tpu as pltpu
 from jax.sharding import PartitionSpec as P
 
 FGROUP = 16
+CHUNK = 128
 
 
 HIGHEST = lax.Precision.HIGHEST
@@ -80,7 +84,7 @@
     return jnp.stack([real_part, imag_part]).reshape(shape)
 
 
-def per_device(sequence, in_weight, short_taps, decay_rates, residues, skip_gain):
+def spread_positions(sequence, in_weight, short_taps, decay_rates, residues, skip_gain):
     whole = lax.all_gather(sequence, "chan", axis=1, tiled=True)
     row_count = whole.shape[0]
     lane_count = in_weight.shape[2]
@@ -149,6 +153,111 @@
     return (query * (conv + skip_gain * signal)).astype(jnp.bfloat16)
 
 
+def operator_kernel(groups, proj_ref, taps_ref, skip_ref, near_ref, into_ref, out_of_ref, decay_ref, mixed_ref):
+    total = proj_ref.shape[2]
+    chunks = total // CHUNK
+    tap_count = taps_ref.shape[2]
+    lane = lax.broadcasted_iota(jnp.int32, (FGROUP, total), 1)
+    for group in range(groups):
+        rows = pl.ds(group * FGROUP, FGROUP)
+        streams = []
+        for slot in range(3):
+            block = proj_ref[slot, rows, :].astype(jnp.float32)
+            taps = taps_ref[slot, rows, :]
+            filtered = taps[:, 0:1] * block
+            for tap in range(1, tap_count):
+                moved = jnp.where(lane >= tap, pltpu.roll(block, tap, 1), 0.0)
+                filtered = filtered + taps[:, tap : tap + 1] * moved
+            streams.append(filtered)
+        query, key, value = streams
+        signal = key * value
+        stacked = jnp.concatenate(
+            [signal[:, a * CHUNK : (a + 1) * CHUNK] for a in range(chunks)], axis=0
+        )
+        near = jnp.dot(stacked, near_ref[group], precision=HIGHEST)
+        added = jnp.dot(stacked, into_ref[group], precision=HIGHEST)
+        decay = decay_ref[group]
+        state = jnp.zeros((FGROUP, added.shape[1]), jnp.float32)
+        states = []
+        for a in range(chunks):
+            states.append(state)
+            state = state * decay + added[a * FGROUP : (a + 1) * FGROUP, :]
+        far = jnp.dot(jnp.concatenate(states, axis=0), out_of_ref[group], precision=HIGHEST)
+        out = near + far
+        conv = jnp.concatenate(
+            [out[a * FGROUP : (a + 1) * FGROUP, :] for a in range(chunks)], axis=1
+        )
+        mixed = query * (conv + skip_ref[rows, :] * signal)
+        mixed_ref[rows, :] = mixed.astype(mixed_ref.dtype)
+
+
+def filter_tables(decay_rates, residues):
+    steps = jnp.arange(CHUNK, dtype=jnp.int32)
+    moments = steps.astype(jnp.float32)
+    weights = residues * jnp.sqrt(2.0 * decay_rates)
+    lag = steps[None, :] - steps[:, None]
+    near = jnp.sum(
+        weights[:, :, None, None]
+        * jnp.exp(-decay_rates[:, :, None, None] * jnp.maximum(lag, 0).astype(jnp.float32)),
+        axis=1,
+    )
+    near = jnp.where(lag >= 0, near, 0.0)
+    into = jnp.exp(-decay_rates[:, None, :] * (CHUNK - 1.0 - moments)[None, :, None])
+    out_of = weights[:, :, None] * jnp.exp(-decay_rates[:, :, None] * (moments + 1.0))
+    decay = jnp.exp(-decay_rates * float(CHUNK))[:, None, :]
+    return near, into, out_of, decay
+
+
+def own_part(array, size, axis):
+    return lax.dynamic_slice_in_dim(array, lax.axis_index("ctx") * size, size, axis)
+
+
+def spread_channels(sequence, in_weight, short_taps, decay_rates, residues, skip_gain):
+    count = lax.axis_size("ctx")
+    halves = lax.axis_size("chan")
+    own_rows, features = sequence.shape
+    slots, own_depth, lanes = in_weight.shape
+    total = own_rows * count
+    own = lanes // count
+    groups = own // FGROUP
+    gathered = lax.all_gather(sequence, ("chan", "ctx"), axis=0, tiled=True)
+    gathered = gathered.reshape(halves, total, features)
+    parts = in_weight.reshape(slots, own_depth, count, own).transpose(2, 0, 3, 1)
+    parts = lax.all_to_all(parts, "ctx", split_axis=0, concat_axis=0, tiled=True)
+    weight = parts.transpose(1, 2, 0, 3).reshape(slots * own, halves, features)
+    tables = filter_tables(
+        own_part(decay_rates, groups, 0), own_part(residues, groups, 0)
+    )
+    taps = own_part(short_taps, own, 2).transpose(0, 2, 1)
+    skip = own_part(skip_gain, own, 0)[:, None]
+    projections = jnp.einsum(
+        "nhd,htd->nt", weight, gathered, preferred_element_type=jnp.float32
+    ).astype(jnp.bfloat16)
+    mixed = pl.pallas_call(
+        functools.partial(operator_kernel, groups),
+        out_shape=jax.ShapeDtypeStruct((own, total), jnp.bfloat16),
+        compiler_params=pltpu.CompilerParams(vmem_limit_bytes=32 * 2**20),
+        name="operator",
+    )(projections.reshape(slots, own, total), taps, skip, *tables)
+    mixed = lax.all_to_all(mixed, "ctx", split_axis=1, concat_axis=0, tiled=True)
+    return mixed.T
+
+
+def per_device(sequence, in_weight, short_taps, decay_rates, residues, skip_gain):
+    count = lax.axis_size("ctx")
+    halves = lax.axis_size("chan")
+    sequence_bytes = sequence.size * count * halves
+    weight_bytes = in_weight.size * count
+    own = in_weight.shape[2] // count
+    by_channel = (
+        sequence_bytes <= weight_bytes
+        and own % FGROUP == 0
+        and sequence.shape[0] * count % CHUNK == 0
+    )
+    plan = spread_channels if by_channel else spread_positions
+    return plan(sequence, in_weight, short_taps, decay_rates, residues, skip_gain)
+
+
 def solution(mesh):
     return jax.shard_map(
         per_device,

time: 342 us -> 186 us (0.54)
  waiting for transfers between devices: 211 us -> 124 us
  starting transfers between devices: 33.6 us -> 7.52 us
  matrix products: 31.9 us -> 12 us
  blocking collectives: 31.7 us -> 13.6 us
  other arithmetic: 5.6 us -> 1.32 us
    all_gather x2 -> x1, waiting for transfers between devices: 146 us -> 82.5 us  [spread_channels(): gathered = lax.all_gather(sequence, ('chan', 'ctx'), axis=0, tiled=True)]
    all_to_all x5 -> x1, starting transfers between devices: 31.4 us -> 7.52 us  [spread_channels(): lax.all_to_all(parts, 'ctx', split_axis=0, concat_axis=0, tiled=True)]
    all_to_all x5 -> x1, waiting for transfers between devices: 63.3 us -> 40.4 us  [spread_channels(): lax.all_to_all(parts, 'ctx', split_axis=0, concat_axis=0, tiled=True)]
    dot_general x25 -> x1, matrix products: 31.9 us -> 12 us  [spread_channels(): jnp.einsum('nhd,htd->nt', weight, gathered, preferred_element_type=jnp.fl...]
    all_to_all x1, blocking collectives: 31.7 us -> 13.6 us  [spread_channels(): lax.all_to_all(mixed, 'ctx', split_axis=1, concat_axis=0, tiled=True)]
    another operation x6 -> x0, local copies, waits for them, and re-layouts: 4.84 us -> none  [the longest x2 1.69 us: rotate_field(): return jnp.stack([real_part, imag_part])]
    transpose x0 -> x3, local copies, waits for them, and re-layouts: none -> 4.14 us  [the longest x1 2.04 us: spread_channels(): weight = parts.transpose(1, 2, 0, 3).reshape(slots * own, halves, features)]
    reshape x1, local copies, waits for them, and re-layouts: 0.2 us -> 3.63 us  [spread_channels(): weight = parts.transpose(1, 2, 0, 3).reshape(slots * own, halves, features)]
  transfers between devices with their start and end apart: 8 -> 2, of which waited for: 7 -> 2; matrix products, arithmetic and copies ran while one was open for 9% -> 6% of each run, Pallas kernels for 0% -> 0%
where the time goes in v1:
time: 186 us
  waiting for transfers between devices  124 us (67%)
  blocking collectives  13.6 us (7%)
  between operations  13.5 us (7%)
  matrix products  12 us (6%)
  local copies, waits for them, and re-layouts  10.8 us (6%)
  starting transfers between devices  7.52 us (4%)
  Pallas kernels  3.13 us (2%)
    all_gather x1, waiting for transfers between devices, spread_channels(): gathered = lax.all_gather(sequence, ('chan', 'ctx'), axis=0, tiled=True)  82.5 us
    all_to_all x1, waiting for transfers between devices, spread_channels(): lax.all_to_all(parts, 'ctx', split_axis=0, concat_axis=0, tiled=True)  40.4 us
    all_to_all x1, blocking collectives, spread_channels(): lax.all_to_all(mixed, 'ctx', split_axis=1, concat_axis=0, tiled=True)  13.6 us
    dot_general x1, matrix products, spread_channels(): jnp.einsum('nhd,htd->nt', weight, gathered, preferred_element_type=jnp.fl...  12 us
    all_to_all x1, starting transfers between devices, spread_channels(): lax.all_to_all(parts, 'ctx', split_axis=0, concat_axis=0, tiled=True)  7.52 us
  transfers between devices with their start and end apart: 2, of which 2 were waited for; matrix products, arithmetic and copies ran while one was open for 6% of the time, Pallas kernels for 0%

profile of v1, /device:TPU:0, one launch (start us, length us, event | category | flops | bytes accessed | tf_op | source)
XLA Modules:
  0.0 185.6 jit_solution(2267468381728967286)
XLA Ops:
  6.5 0.7 all-gather.2.cloned.1.call-update
  7.3 1.7 copy.61
  9.0 1.2 copy.62
  10.2 7.5 %all-to-all-start = ((bf16[16,3,64,256]{3,2,1,0:T(8,128)(2,1)}), bf16[16,3,64,256]{3,2,1,0:T(8,128)(2,1)S(1)}, u32[]{:S(2)}, u32[]{:S(2)}) async-start(bf16[16,3,64,256]{3,2,1,0:T(8,128)(2,1)} %copy.62), calls=%async_computation | async-start | bytes 3145728 | tf_op jit(solution)/shard_map/all_to_all | solution.py:226
  17.8 0.0 copy-done.1
  17.8 0.1 constant_dynamic-slice_fusion
  17.9 0.1 copy.73
  17.9 0.1 copy.74
  18.0 0.1 constant_dynamic-slice_fusion.2
  18.1 0.1 copy.72
  18.2 0.8 dynamic-slice_bitcast_fusion
  19.0 0.1 copy.68.skip_ref
  19.2 1.0 multiply_reduce_fusion
  20.2 0.1 exponential_multiply_fusion.out_of_ref
  20.3 0.1 multiply_exponential_fusion.into_ref
  20.4 40.4 %all-to-all-done = bf16[16,3,64,256]{3,2,1,0:T(8,128)(2,1)S(1)} async-done(((bf16[16,3,64,256]{3,2,1,0:T(8,128)(2,1)}), bf16[16,3,64,256]{3,2,1,0:T(8,128)(2,1)S(1)}, u32[]{:S(2)}, u32[]{:S(2)}) %all-to-all-start) | async-done | bytes 1572896 | tf_op jit(solution)/shard_map/all_to_all | solution.py:226
  60.9 2.0 %copy.63 = bf16[3,64,16,256]{3,2,1,0:T(8,128)(2,1)} copy(bf16[3,64,16,256]{3,1,0,2:T(8,128)(2,1)S(1)} %bitcast.32) | data formatting | bytes 3145728 | tf_op jit(solution)/shard_map/transpose | solution.py:227
  62.9 3.6 %reshape.48 = bf16[192,2,2048]{2,1,0:T(2,128)(2,1)} reshape(bf16[3,64,16,256]{3,2,1,0:T(8,128)(2,1)} %copy.63) | data formatting | bytes 3145728 | tf_op jit(solution)/shard_map/reshape | solution.py:227
  66.5 82.5 %all-gather.2.cloned.1.call-done = bf16[4096,2048]{1,0:T(8,128)(2,1)} async-done(((bf16[128,2048]{1,0:T(8,128)(2,1)}), bf16[4096,2048]{1,0:T(8,128)(2,1)}) %all-gather.2.cloned.1.call-update) | async-done | bytes 16777232 | tf_op jit(solution)/shard_map/all_gather | solution.py:223
  149.1 12.0 %fusion = bf16[192,2048]{1,0:T(8,128)(2,1)S(1)} fusion(bf16[2,2048,2048]{2,1,0:T(8,128)(2,1)} %bitcast.35, bf16[192,2,2048]{2,1,0:T(2,128)(2,1)} %reshape.48), kind=kOutput, calls=%fused_computation.2 | convolution fusion | flops 3221618688 | bytes 19136512 | tf_op jit(solution)/shard_map/nhd,htd->nt/dot_general | solution.py:233
  161.1 3.1 %operator.1 = bf16[64,2048]{1,0:T(8,128)(2,1)S(1)} custom-call(bf16[3,64,2048]{2,1,0:T(8,128)(2,1)S(1)} %bitcast.29, f32[3,64,7]{2,1,0:T(8,128)S(1)} %bitcast.30, f32[64,1]{1,0:T(8,128)S(1)} %copy.68.skip_ref, f32[4,128,128]{2,1,0:T(8,128)S(1)} %broadcast_select_fusion.near_ref, f32[4,128,16]{2,1,0:T(8,128)S(1)} %multiply_exponential_fusion.into_ref, ...), custom_call_target="tpu_custom_call" | custom-call | tf_op jit(solution)/shard_map/operator/pallas_call | solution.py:236
  164.2 0.1 copy_bitcast_fusion
  164.3 13.6 %all_to_all.24 = bf16[64,16,128]{2,0,1:T(8,128)(2,1)S(1)} all-to-all(bf16[64,16,128]{2,0,1:T(8,128)(2,1)S(1)} %copy_bitcast_fusion), channel_id=1, replica_groups=mesh['ctx'=16,'chan'=2] {'ctx'}, dimensions={1} | all-to-all | bytes 524288 | tf_op jit(solution)/shard_map/all_to_all | solution.py:242
  177.9 0.8 copy.71
  (12 shorter events, 0.1 us)
Async XLA Ops:
  6.5 11.5 %copy-start = (f32[3,7,1024]{2,1,0:T(8,128)S(1)}, f32[3,7,1024]{2,1,0:T(8,128)}, u32[]{:S(2)}) copy-start(f32[3,7,1024]{2,1,0:T(8,128)} %param.8) | copy-start | bytes 258052
  6.5 142.6 %all-gather.2.cloned.1.call-start = ((), (), s32[]{:S(2)}) async-start(), calls=%async_computation.2 | async-start | bytes 17301504 | tf_op jit(solution)/shard_map/all_gather | solution.py:223
  10.2 7.5 %copy-start.1 = (f32[64,16]{0,1:T(8,128)S(1)}, f32[64,16]{0,1:T(8,128)}, u32[]{:S(2)}) copy-start(f32[64,16]{0,1:T(8,128)} %param.9) | copy-start | bytes 12292
  10.2 7.5 %copy-start.2 = (f32[64,16]{0,1:T(8,128)S(1)}, f32[64,16]{0,1:T(8,128)}, u32[]{:S(2)}) copy-start(f32[64,16]{0,1:T(8,128)} %param.10) | copy-start | bytes 12292
  10.2 50.6 %all-to-all-start = ((bf16[16,3,64,256]{3,2,1,0:T(8,128)(2,1)}), bf16[16,3,64,256]{3,2,1,0:T(8,128)(2,1)S(1)}, u32[]{:S(2)}, u32[]{:S(2)}) async-start(bf16[16,3,64,256]{3,2,1,0:T(8,128)(2,1)} %copy.62), calls=%async_computation | async-start | bytes 3145728 | tf_op jit(solution)/shard_map/all_to_all | solution.py:226
Sparse Core Ops, SparseCore 0:
  10.2 138.7 all-gather.1

commit v2 on v1

--- a/solution.py
+++ b/solution.py
@@ -191,6 +191,246 @@
         mixed_ref[rows, :] = mixed.astype(mixed_ref.dtype)
 
 
+MESH = pl.DeviceIdType.MESH
+PIECE = 32
+CORES = 2
+SIDE = 2
+
+
+def gather_kernel(count, seq_ref, parts_ref, proj_ref, held, weight, w_send, w_recv, send, recv):
+    me = lax.axis_index("ctx")
+    x = lax.axis_index("chan")
+    core = me % CORES
+    y = me // CORES % SIDE
+    z = me // (CORES * SIDE)
+    depth_z = count // (CORES * SIDE)
+    rows = seq_ref.shape[0]
+    pieces = rows // PIECE
+    depth = parts_ref.shape[2]
+    per_half = count // 2
+
+    def ctx_of(zz, yy, cc):
+        return (zz * SIDE + yy) * CORES + cc
+
+    barrier = pltpu.get_barrier_semaphore()
+
+    def greet(step, carry):
+        pl.semaphore_signal(
+            barrier, inc=1, device_id=((me + step) % count, x), device_id_type=MESH
+        )
+        return carry
+
+    lax.fori_loop(1, count, greet, 0)
+    pl.semaphore_signal(barrier, inc=1, device_id=(me, 1 - x), device_id_type=MESH)
+    pl.semaphore_wait(barrier, count)
+
+    def weight_copy(part, source, target):
+        lanes = pl.ds(pl.multiple_of(source % per_half * depth, depth), depth)
+        return pltpu.make_async_remote_copy(
+            src_ref=parts_ref.at[part],
+            dst_ref=weight.at[source // per_half, :, lanes],
+            send_sem=w_send.at[part],
+            recv_sem=w_recv.at[source],
+            device_id=(target, x),
+            device_id_type=MESH,
+        )
+
+    def piece_copy(xx, block, piece, kind, target):
+        where = held.at[xx, pl.ds(pl.multiple_of(block * rows + piece * PIECE, PIECE), PIECE), :]
+        return pltpu.make_async_remote_copy(
+            src_ref=where,
+            dst_ref=where,
+            send_sem=send.at[kind, xx, block, piece],
+            recv_sem=recv.at[xx, block, piece],
+            device_id=target,
+            device_id_type=MESH,
+        )
+
+    def first_hop(piece):
+        late = piece // (pieces - 1)
+        return (1 - late) * (1 - y) + late * y, (1 - late) * x + late * (1 - x)
+
+    def second_hop(piece):
+        late = piece // (pieces - 1)
+        return late * (1 - y) + (1 - late) * y, late * x + (1 - late) * (1 - x)
+
+    sibling = (ctx_of(z, y, 1 - core), x)
+
+    def valid(d):
+        return (z + d >= 0) & (z + d < depth_z)
+
+    def send_on(d, piece, act):
+        block = ctx_of(z + d, y, core)
+        if d >= 0:
+            @pl.when(z > 0)
+            def _():
+                act(piece_copy(x, block, piece, 0, (ctx_of(z - 1, y, core), x)))
+        if d <= 0:
+            @pl.when(z < depth_z - 1)
+            def _():
+                act(piece_copy(x, block, piece, 1, (ctx_of(z + 1, y, core), x)))
+        yy, xx = first_hop(piece)
+        act(piece_copy(x, block, piece, 2, (ctx_of(z, yy, core), xx)))
+        yy, xx = second_hop(piece)
+        act(piece_copy(x, block, piece, 3, (ctx_of(z, yy, core), xx)))
+        act(piece_copy(x, block, piece, 4, sibling))
+
+    def send_turned(d, piece, act):
+        yy, xx = first_hop(piece)
+        block = ctx_of(z + d, yy, core)
+        y2, x2 = second_hop(piece)
+        act(piece_copy(xx, block, piece, 3, (ctx_of(z, y2, core), x2)))
+        act(piece_copy(xx, block, piece, 4, sibling))
+
+    def send_last(d, piece, act):
+        y2, x2 = second_hop(piece)
+        act(piece_copy(x2, ctx_of(z + d, y2, core), piece, 4, sibling))
+        act(piece_copy(1 - x, ctx_of(z + d, 1 - y, core), piece, 4, sibling))
+
+    def arrived(xx, block, piece):
+        piece_copy(xx, block, piece, 4, sibling).wait_recv()
+
+    def each_piece(d, body):
+        @pl.when(valid(d))
+        def _():
+            def step(piece, carry):
+                body(piece)
+                return carry
+            lax.fori_loop(0, pieces, step, 0)
+
+    def start(copy):
+        copy.start()
+
+    def finish(copy):
+        copy.wait_send()
+
+    def stage_line(d):
+        def body(piece):
+            if d != 0:
+                arrived(x, ctx_of(z + d, y, core), piece)
+            send_on(d, piece, start)
+        each_piece(d, body)
+
+    def stage_turned(d):
+        def body(piece):
+            yy, xx = first_hop(piece)
+            arrived(xx, ctx_of(z + d, yy, core), piece)
+            send_turned(d, piece, start)
+        each_piece(d, body)
+
+    def stage_last(d):
+        def body(piece):
+            y2, x2 = second_hop(piece)
+            arrived(x2, ctx_of(z + d, y2, core), piece)
+            arrived(1 - x, ctx_of(z + d, 1 - y, core), piece)
+            send_last(d, piece, start)
+        each_piece(d, body)
+
+    def multiply(d):
+        def body(piece):
+            for yy in range(SIDE):
+                for xx in range(2):
+                    arrived(xx, ctx_of(z + d, yy, 1 - core), piece)
+        each_piece(d, body)
+
+        @pl.when(valid(d))
+        def _():
+            width = CORES * rows
+            def step(yy, carry):
+                span = pl.ds(pl.multiple_of(ctx_of(z + d, yy, 0) * rows, width), width)
+                out = jnp.zeros((weight.shape[1], width), jnp.float32)
+                for xx in range(2):
+                    out = out + lax.dot_general(
+                        weight[xx], held[xx, span, :], (((1,), (1,)), ((), ())),
+                        preferred_element_type=jnp.float32,
+                    )
+                proj_ref[:, span] = out.astype(proj_ref.dtype)
+                return carry
+            lax.fori_loop(0, SIDE, step, 0)
+
+    held[x, pl.ds(pl.multiple_of(me * rows, rows), rows), :] = seq_ref[...]
+    stage_line(0)
+
+    def send_weight(step, carry):
+        target = (me + step) % count
+        weight_copy(target, me, target).start()
+        return carry
+
+    lax.fori_loop(1, count, send_weight, 0)
+    own = pl.ds(pl.multiple_of(me % per_half * depth, depth), depth)
+    weight[me // per_half, :, own] = parts_ref[me]
+
+    order = [0]
+    for far in range(1, depth_z):
+        order += [far, -far]
+    for d in order[1:3]:
+        stage_line(d)
+    stage_turned(order[0])
+    for d in order[3:5]:
+        stage_line(d)
+    for d in order[1:3]:
+        stage_turned(d)
+    stage_last(order[0])
+    for d in order[5:]:
+        stage_line(d)
+    for d in order[3:5]:
+        stage_turned(d)
+    for d in order[1:3]:
+        stage_last(d)
+    for d in order[5:]:
+        stage_turned(d)
+
+    def take_weight(step, carry):
+        source = (me + step) % count
+        weight_copy(source, source, source).wait_recv()
+        return carry
+
+    lax.fori_loop(1, count, take_weight, 0)
+    for d in order[3:5]:
+        stage_last(d)
+    for d in order[:3]:
+        multiply(d)
+    for d in order[5:]:
+        stage_last(d)
+    for d in order[3:]:
+        multiply(d)
+
+    def sent_weight(step, carry):
+        target = (me + step) % count
+        weight_copy(target, me, target).wait_send()
+        return carry
+
+    lax.fori_loop(1, count, sent_weight, 0)
+    for d in order:
+        each_piece(d, lambda piece: send_on(d, piece, finish))
+        each_piece(d, lambda piece: send_turned(d, piece, finish))
+        each_piece(d, lambda piece: send_last(d, piece, finish))
+
+
+def gather_project(sequence, parts, count):
+    rows, features = sequence.shape
+    own, depth = parts.shape[1:]
+    pieces = rows // PIECE
+    return pl.pallas_call(
+        functools.partial(gather_kernel, count),
+        out_shape=jax.ShapeDtypeStruct((own, rows * count), jnp.bfloat16),
+        in_specs=[pl.BlockSpec(memory_space=pltpu.VMEM)] * 2,
+        out_specs=pl.BlockSpec(memory_space=pltpu.VMEM),
+        scratch_shapes=[
+            pltpu.VMEM((2, count * rows, features), jnp.bfloat16),
+            pltpu.VMEM((2, own, features), jnp.bfloat16),
+            pltpu.SemaphoreType.DMA((count,)),
+            pltpu.SemaphoreType.DMA((count,)),
+            pltpu.SemaphoreType.DMA((5, 2, count, pieces)),
+            pltpu.SemaphoreType.DMA((2, count, pieces)),
+        ],
+        compiler_params=pltpu.CompilerParams(
+            collective_id=0, has_side_effects=True, vmem_limit_bytes=40 * 2**20
+        ),
+        name="gather_project",
+    )(sequence, parts)
+
+
 def filter_tables(decay_rates, residues):
     steps = jnp.arange(CHUNK, dtype=jnp.int32)
     moments = steps.astype(jnp.float32)
@@ -214,25 +454,19 @@
 
 def spread_channels(sequence, in_weight, short_taps, decay_rates, residues, skip_gain):
     count = lax.axis_size("ctx")
-    halves = lax.axis_size("chan")
     own_rows, features = sequence.shape
     slots, own_depth, lanes = in_weight.shape
     total = own_rows * count
     own = lanes // count
     groups = own // FGROUP
-    gathered = lax.all_gather(sequence, ("chan", "ctx"), axis=0, tiled=True)
-    gathered = gathered.reshape(halves, total, features)
     parts = in_weight.reshape(slots, own_depth, count, own).transpose(2, 0, 3, 1)
-    parts = lax.all_to_all(parts, "ctx", split_axis=0, concat_axis=0, tiled=True)
-    weight = parts.transpose(1, 2, 0, 3).reshape(slots * own, halves, features)
+    parts = parts.reshape(count, slots * own, own_depth)
     tables = filter_tables(
         own_part(decay_rates, groups, 0), own_part(residues, groups, 0)
     )
     taps = own_part(short_taps, own, 2).transpose(0, 2, 1)
     skip = own_part(skip_gain, own, 0)[:, None]
-    projections = jnp.einsum(
-        "nhd,htd->nt", weight, gathered, preferred_element_type=jnp.float32
-    ).astype(jnp.bfloat16)
+    projections = gather_project(sequence, parts, count)
     mixed = pl.pallas_call(
         functools.partial(operator_kernel, groups),
         out_shape=jax.ShapeDtypeStruct((own, total), jnp.bfloat16),
@@ -252,6 +486,10 @@
     by_channel = (
         sequence_bytes <= weight_bytes
         and own % FGROUP == 0
+        and halves == 2
+        and count % (CORES * SIDE * 2) == 0
+        and sequence.shape[0] % (2 * PIECE) == 0
+        and in_weight.shape[1] * count == sequence.shape[1] * halves
         and sequence.shape[0] * count % CHUNK == 0
     )
     plan = spread_channels if by_channel else spread_positions

time: 186 us -> 131 us (0.70)
  waiting for transfers between devices: 124 us -> 0 us
  Pallas kernels: 3.13 us -> 112 us
  between operations: 13.5 us -> 0.15 us
  matrix products: 12 us -> 0 us
  starting transfers between devices: 7.52 us -> 0 us
  local copies, waits for them, and re-layouts: 10.8 us -> 4.1 us
    pallas_call x0 -> x1, Pallas kernels: none -> 109 us  [gather_project(): pl.pallas_call(functools.partial(gather_kernel, count), out_shape=jax.Sha...]
    all_gather x1 -> x0, waiting for transfers between devices: 82.5 us -> none  [spread_channels(): gathered = lax.all_gather(sequence, ('chan', 'ctx'), axis=0, tiled=True)]
    all_to_all x1 -> x0, waiting for transfers between devices: 40.4 us -> none  [spread_channels(): lax.all_to_all(parts, 'ctx', split_axis=0, concat_axis=0, tiled=True)]
    dot_general x1 -> x0, matrix products: 12 us -> none  [spread_channels(): jnp.einsum('nhd,htd->nt', weight, gathered, preferred_element_type=jnp.fl...]
    all_to_all x1 -> x0, starting transfers between devices: 7.52 us -> none  [spread_channels(): lax.all_to_all(parts, 'ctx', split_axis=0, concat_axis=0, tiled=True)]
    reshape x1 -> x0, local copies, waits for them, and re-layouts: 3.63 us -> none  [spread_channels(): weight = parts.transpose(1, 2, 0, 3).reshape(slots * own, halves, features)]
    transpose x1 -> x0, local copies, waits for them, and re-layouts: 2.04 us -> none  [spread_channels(): weight = parts.transpose(1, 2, 0, 3).reshape(slots * own, halves, features)]
  transfers between devices with their start and end apart: 2 -> 0, of which waited for: 2 -> 0; matrix products, arithmetic and copies ran while one was open for 6% -> 0% of each run, Pallas kernels for 0% -> 0%
where the time goes in v2:
time: 131 us
  Pallas kernels  112 us (85%)
  blocking collectives  13.6 us (10%)
  local copies, waits for them, and re-layouts  4.1 us (3%)
  other arithmetic  1.32 us (1%)
    pallas_call x1, Pallas kernels, gather_project(): pl.pallas_call(functools.partial(gather_kernel, count), out_shape=jax.Sha...  109 us
    all_to_all x1, blocking collectives, spread_channels(): lax.all_to_all(mixed, 'ctx', split_axis=1, concat_axis=0, tiled=True)  13.6 us
    pallas_call x1, Pallas kernels, spread_channels(): pl.pallas_call(functools.partial(operator_kernel, groups), out_shape=jax....  3.11 us

profile of v2, /device:TPU:0, one launch (start us, length us, event | category | flops | bytes accessed | tf_op | source)
XLA Modules:
  0.0 131.2 jit_solution(11717344886416303680)
XLA Ops:
  0.0 0.0 copy-start
  0.1 1.7 %copy.44 = bf16[3,256,1024]{1,2,0:T(8,128)(2,1)S(1)} copy(bf16[3,256,1024]{2,1,0:T(8,128)(2,1)} %param.7) | data formatting | bytes 3145728 | tf_op args[1]
  1.8 0.0 copy-start.2
  1.8 0.0 copy-start.3
  1.8 0.2 copy.45
  2.0 0.0 copy-start.1
  2.0 0.0 copy-done
  2.0 0.1 constant_dynamic-slice_fusion.2
  2.1 0.1 copy.53
  2.2 0.8 dynamic-slice_bitcast_fusion
  3.0 0.1 copy.49.skip_ref
  3.1 0.0 copy-done.2
  3.1 0.1 constant_dynamic-slice_fusion
  3.2 0.1 copy.55
  3.2 0.1 copy.54
  3.3 0.1 multiply_exponential_fusion.into_ref
  3.4 1.0 multiply_reduce_fusion
  4.5 0.1 exponential_multiply_fusion.out_of_ref
  4.6 0.0 copy-done.1
  4.6 108.9 %gather_project.1 = bf16[192,2048]{1,0:T(8,128)(2,1)S(1)} custom-call(bf16[128,2048]{1,0:T(8,128)(2,1)S(1)} %copy-done.1, bf16[16,192,256]{2,1,0:T(8,128)(2,1)S(1)} %bitcast.21), custom_call_target="tpu_custom_call" | custom-call | tf_op jit(solution)/shard_map/gather_project/pallas_call | solution.py:414
  113.6 3.1 %operator.1 = bf16[64,2048]{1,0:T(8,128)(2,1)S(1)} custom-call(bf16[3,64,2048]{2,1,0:T(8,128)(2,1)S(1)} %bitcast.22, f32[3,64,7]{2,1,0:T(8,128)S(1)} %bitcast.23, f32[64,1]{1,0:T(8,128)S(1)} %copy.49.skip_ref, f32[4,128,128]{2,1,0:T(8,128)S(1)} %broadcast_select_fusion.near_ref, f32[4,128,16]{2,1,0:T(8,128)S(1)} %multiply_exponential_fusion.into_ref, ...), custom_call_target="tpu_custom_call" | custom-call | tf_op jit(solution)/shard_map/operator/pallas_call | solution.py:470
  116.7 0.1 copy_bitcast_fusion
  116.7 13.6 %all_to_all.19 = bf16[64,16,128]{2,0,1:T(8,128)(2,1)S(1)} all-to-all(bf16[64,16,128]{2,0,1:T(8,128)(2,1)S(1)} %copy_bitcast_fusion), channel_id=1, replica_groups=mesh['ctx'=16,'chan'=2] {'ctx'}, dimensions={1} | all-to-all | bytes 524288 | tf_op jit(solution)/shard_map/all_to_all | solution.py:476
  130.3 0.8 copy.52
  (7 shorter events, 0.1 us)
Async XLA Ops:
  0.0 2.0 %copy-start = (f32[3,7,1024]{2,1,0:T(8,128)S(1)}, f32[3,7,1024]{2,1,0:T(8,128)}, u32[]{:S(2)}) copy-start(f32[3,7,1024]{2,1,0:T(8,128)} %param.8) | copy-start | bytes 258052
  1.8 1.3 copy-start.2
  1.8 1.3 copy-start.3
  2.0 2.6 %copy-start.1 = (bf16[128,2048]{1,0:T(8,128)(2,1)S(1)}, bf16[128,2048]{1,0:T(8,128)(2,1)}, u32[]{:S(2)}) copy-start(bf16[128,2048]{1,0:T(8,128)(2,1)} %seq_ref.1) | copy-start | bytes 1572868

commit v3 on v2

--- a/solution.py
+++ b/solution.py
@@ -153,8 +153,8 @@
     return (query * (conv + skip_gain * signal)).astype(jnp.bfloat16)
 
 
-def operator_kernel(groups, proj_ref, taps_ref, skip_ref, near_ref, into_ref, out_of_ref, decay_ref, mixed_ref):
-    total = proj_ref.shape[2]
+def operate(groups, sums, taps_ref, skip_ref, near_ref, into_ref, out_of_ref, decay_ref, mixed_ref):
+    own, total = mixed_ref.shape
     chunks = total // CHUNK
     tap_count = taps_ref.shape[2]
     lane = lax.broadcasted_iota(jnp.int32, (FGROUP, total), 1)
@@ -162,7 +162,8 @@
         rows = pl.ds(group * FGROUP, FGROUP)
         streams = []
         for slot in range(3):
-            block = proj_ref[slot, rows, :].astype(jnp.float32)
+            block = sums[pl.ds(slot * own + group * FGROUP, FGROUP), :]
+            block = block.astype(jnp.bfloat16).astype(jnp.float32)
             taps = taps_ref[slot, rows, :]
             filtered = taps[:, 0:1] * block
             for tap in range(1, tap_count):
@@ -197,7 +198,11 @@
 SIDE = 2
 
 
-def gather_kernel(count, seq_ref, parts_ref, proj_ref, held, weight, w_send, w_recv, send, recv):
+def gather_kernel(
+    count, groups, seq_ref, parts_ref, taps_ref, skip_ref, near_ref, into_ref, out_of_ref, decay_ref,
+    out_ref, held, weight, kept, given, taken, mixed,
+    w_send, w_recv, send, recv, p_send, p_recv, o_send, o_recv,
+):
     me = lax.axis_index("ctx")
     x = lax.axis_index("chan")
     core = me % CORES
@@ -206,8 +211,10 @@
     depth_z = count // (CORES * SIDE)
     rows = seq_ref.shape[0]
     pieces = rows // PIECE
-    depth = parts_ref.shape[2]
+    own, depth = parts_ref.shape[1:]
     per_half = count // 2
+    width = CORES * rows
+    half = me // per_half
 
     def ctx_of(zz, yy, cc):
         return (zz * SIDE + yy) * CORES + cc
@@ -215,46 +222,50 @@
     barrier = pltpu.get_barrier_semaphore()
 
     def greet(step, carry):
-        pl.semaphore_signal(
-            barrier, inc=1, device_id=((me + step) % count, x), device_id_type=MESH
-        )
+        target = (me + step) % count
+        pl.semaphore_signal(barrier, inc=1, device_id=(target, x), device_id_type=MESH)
+        pl.semaphore_signal(barrier, inc=1, device_id=(target, 1 - x), device_id_type=MESH)
         return carry
 
     lax.fori_loop(1, count, greet, 0)
     pl.semaphore_signal(barrier, inc=1, device_id=(me, 1 - x), device_id_type=MESH)
-    pl.semaphore_wait(barrier, count)
-
-    def weight_copy(part, source, target):
+    pl.semaphore_wait(barrier, 2 * count - 1)
+
+    def weight_copy(part, source, column, target):
         lanes = pl.ds(pl.multiple_of(source % per_half * depth, depth), depth)
         return pltpu.make_async_remote_copy(
             src_ref=parts_ref.at[part],
-            dst_ref=weight.at[source // per_half, :, lanes],
+            dst_ref=weight.at[column, :, lanes],
             send_sem=w_send.at[part],
-            recv_sem=w_recv.at[source],
+            recv_sem=w_recv.at[column, source % per_half],
+            device_id=target,
+            device_id_type=MESH,
+        )
+
+    def each_target(act):
+        def step(index, carry):
+            target = (me + index) % count
+            act(weight_copy(target, me, x, (target, half)))
+            return carry
+
+        lax.fori_loop(1, count, step, 0)
+
+        @pl.when(half != x)
+        def _():
+            act(weight_copy(me, me, x, (me, half)))
+
+    def piece_copy(block, piece, kind, target):
+        where = held.at[pl.ds(pl.multiple_of(block * rows + piece * PIECE, PIECE), PIECE), :]
+        return pltpu.make_async_remote_copy(
+            src_ref=where,
+            dst_ref=where,
+            send_sem=send.at[kind, block, piece],
+            recv_sem=recv.at[block, piece],
             device_id=(target, x),
             device_id_type=MESH,
         )
 
-    def piece_copy(xx, block, piece, kind, target):
-        where = held.at[xx, pl.ds(pl.multiple_of(block * rows + piece * PIECE, PIECE), PIECE), :]
-        return pltpu.make_async_remote_copy(
-            src_ref=where,
-            dst_ref=where,
-            send_sem=send.at[kind, xx, block, piece],
-            recv_sem=recv.at[xx, block, piece],
-            device_id=target,
-            device_id_type=MESH,
-        )
-
-    def first_hop(piece):
-        late = piece // (pieces - 1)
-        return (1 - late) * (1 - y) + late * y, (1 - late) * x + late * (1 - x)
-
-    def second_hop(piece):
-        late = piece // (pieces - 1)
-        return late * (1 - y) + (1 - late) * y, late * x + (1 - late) * (1 - x)
-
-    sibling = (ctx_of(z, y, 1 - core), x)
+    sibling = ctx_of(z, y, 1 - core)
 
     def valid(d):
         return (z + d >= 0) & (z + d < depth_z)
@@ -264,31 +275,19 @@
         if d >= 0:
             @pl.when(z > 0)
             def _():
-                act(piece_copy(x, block, piece, 0, (ctx_of(z - 1, y, core), x)))
+                act(piece_copy(block, piece, 0, ctx_of(z - 1, y, core)))
         if d <= 0:
             @pl.when(z < depth_z - 1)
             def _():
-                act(piece_copy(x, block, piece, 1, (ctx_of(z + 1, y, core), x)))
-        yy, xx = first_hop(piece)
-        act(piece_copy(x, block, piece, 2, (ctx_of(z, yy, core), xx)))
-        yy, xx = second_hop(piece)
-        act(piece_copy(x, block, piece, 3, (ctx_of(z, yy, core), xx)))
-        act(piece_copy(x, block, piece, 4, sibling))
+                act(piece_copy(block, piece, 1, ctx_of(z + 1, y, core)))
+        act(piece_copy(block, piece, 2, ctx_of(z, 1 - y, core)))
+        act(piece_copy(block, piece, 3, sibling))
 
     def send_turned(d, piece, act):
-        yy, xx = first_hop(piece)
-        block = ctx_of(z + d, yy, core)
-        y2, x2 = second_hop(piece)
-        act(piece_copy(xx, block, piece, 3, (ctx_of(z, y2, core), x2)))
-        act(piece_copy(xx, block, piece, 4, sibling))
-
-    def send_last(d, piece, act):
-        y2, x2 = second_hop(piece)
-        act(piece_copy(x2, ctx_of(z + d, y2, core), piece, 4, sibling))
-        act(piece_copy(1 - x, ctx_of(z + d, 1 - y, core), piece, 4, sibling))
-
-    def arrived(xx, block, piece):
-        piece_copy(xx, block, piece, 4, sibling).wait_recv()
+        act(piece_copy(ctx_of(z + d, 1 - y, core), piece, 3, sibling))
+
+    def arrived(block, piece):
+        piece_copy(block, piece, 3, sibling).wait_recv()
 
     def each_piece(d, body):
         @pl.when(valid(d))
@@ -296,6 +295,7 @@
             def step(piece, carry):
                 body(piece)
                 return carry
+
             lax.fori_loop(0, pieces, step, 0)
 
     def start(copy):
@@ -307,58 +307,55 @@
     def stage_line(d):
         def body(piece):
             if d != 0:
-                arrived(x, ctx_of(z + d, y, core), piece)
+                arrived(ctx_of(z + d, y, core), piece)
             send_on(d, piece, start)
+
         each_piece(d, body)
 
     def stage_turned(d):
         def body(piece):
-            yy, xx = first_hop(piece)
-            arrived(xx, ctx_of(z + d, yy, core), piece)
+            arrived(ctx_of(z + d, 1 - y, core), piece)
             send_turned(d, piece, start)
+
         each_piece(d, body)
 
-    def stage_last(d):
-        def body(piece):
-            y2, x2 = second_hop(piece)
-            arrived(x2, ctx_of(z + d, y2, core), piece)
-            arrived(1 - x, ctx_of(z + d, 1 - y, core), piece)
-            send_last(d, piece, start)
-        each_piece(d, body)
-
-    def multiply(d):
-        def body(piece):
-            for yy in range(SIDE):
-                for xx in range(2):
-                    arrived(xx, ctx_of(z + d, yy, 1 - core), piece)
-        each_piece(d, body)
+    def columns(pair):
+        return pl.ds(pl.multiple_of(pair * width, width), width)
+
+    def partial_copy(pair):
+        return pltpu.make_async_remote_copy(
+            src_ref=given.at[:, columns(pair)],
+            dst_ref=taken.at[:, columns(pair)],
+            send_sem=p_send.at[pair],
+            recv_sem=p_recv.at[pair],
+            device_id=(me, 1 - x),
+            device_id_type=MESH,
+        )
+
+    def multiply(d, side):
+        yy = y if side == 0 else 1 - y
+        each_piece(d, lambda piece: arrived(ctx_of(z + d, yy, 1 - core), piece))
 
         @pl.when(valid(d))
         def _():
-            width = CORES * rows
-            def step(yy, carry):
-                span = pl.ds(pl.multiple_of(ctx_of(z + d, yy, 0) * rows, width), width)
-                out = jnp.zeros((weight.shape[1], width), jnp.float32)
-                for xx in range(2):
-                    out = out + lax.dot_general(
-                        weight[xx], held[xx, span, :], (((1,), (1,)), ((), ())),
-                        preferred_element_type=jnp.float32,
-                    )
-                proj_ref[:, span] = out.astype(proj_ref.dtype)
-                return carry
-            lax.fori_loop(0, SIDE, step, 0)
-
-    held[x, pl.ds(pl.multiple_of(me * rows, rows), rows), :] = seq_ref[...]
+            pair = (z + d) * SIDE + yy
+            block = held[columns(pair), :]
+            for column, into in ((1 - x, given), (x, kept)):
+                into[:, columns(pair)] = lax.dot_general(
+                    weight[column], block, (((1,), (1,)), ((), ())),
+                    preferred_element_type=jnp.float32,
+                )
+                if into is given:
+                    partial_copy(pair).start()
+
+    held[pl.ds(pl.multiple_of(me * rows, rows), rows), :] = seq_ref[...]
     stage_line(0)
-
-    def send_weight(step, carry):
-        target = (me + step) % count
-        weight_copy(target, me, target).start()
-        return carry
-
-    lax.fori_loop(1, count, send_weight, 0)
-    own = pl.ds(pl.multiple_of(me % per_half * depth, depth), depth)
-    weight[me // per_half, :, own] = parts_ref[me]
+    each_target(start)
+
+    @pl.when(half == x)
+    def _():
+        lanes = pl.ds(pl.multiple_of(me % per_half * depth, depth), depth)
+        weight[x, :, lanes] = parts_ref[me]
 
     order = [0]
     for far in range(1, depth_z):
@@ -370,65 +367,117 @@
         stage_line(d)
     for d in order[1:3]:
         stage_turned(d)
-    stage_last(order[0])
     for d in order[5:]:
         stage_line(d)
     for d in order[3:5]:
         stage_turned(d)
-    for d in order[1:3]:
-        stage_last(d)
+
+    def take_weight(step, carry):
+        source = x * per_half + step % per_half
+        column = step // per_half
+
+        @pl.when((source != me) | (column != x))
+        def _():
+            weight_copy(source, source, column, (me, 1 - x)).wait_recv()
+
+        return carry
+
+    lax.fori_loop(0, count, take_weight, 0)
+    for d in order[:3]:
+        multiply(d, 0)
+    for d in order[:3]:
+        multiply(d, 1)
+    for d in order[3:5]:
+        multiply(d, 0)
     for d in order[5:]:
         stage_turned(d)
-
-    def take_weight(step, carry):
-        source = (me + step) % count
-        weight_copy(source, source, source).wait_recv()
+    for d in order[3:5]:
+        multiply(d, 1)
+    for d in order[5:]:
+        multiply(d, 0)
+        multiply(d, 1)
+
+    def join(pair, carry):
+        partial_copy(pair).wait_recv()
+        kept[:, columns(pair)] = kept[:, columns(pair)] + taken[:, columns(pair)]
         return carry
 
-    lax.fori_loop(1, count, take_weight, 0)
-    for d in order[3:5]:
-        stage_last(d)
-    for d in order[:3]:
-        multiply(d)
-    for d in order[5:]:
-        stage_last(d)
-    for d in order[3:]:
-        multiply(d)
-
-    def sent_weight(step, carry):
+    lax.fori_loop(0, count // CORES, join, 0)
+    operate(groups, kept, taps_ref, skip_ref, near_ref, into_ref, out_of_ref, decay_ref, mixed)
+    lanes = mixed.shape[0]
+
+    def out_copy(part, source, target):
+        return pltpu.make_async_remote_copy(
+            src_ref=mixed.at[:, pl.ds(pl.multiple_of(part * rows, rows), rows)],
+            dst_ref=out_ref.at[pl.ds(pl.multiple_of(source * lanes, lanes), lanes), :],
+            send_sem=o_send.at[part],
+            recv_sem=o_recv.at[source],
+            device_id=(target, x),
+            device_id_type=MESH,
+        )
+
+    def send_out(step, carry):
         target = (me + step) % count
-        weight_copy(target, me, target).wait_send()
+        out_copy(target, me, target).start()
         return carry
 
-    lax.fori_loop(1, count, sent_weight, 0)
+    lax.fori_loop(1, count, send_out, 0)
+    out_ref[pl.ds(pl.multiple_of(me * lanes, lanes), lanes), :] = mixed[
+        :, pl.ds(pl.multiple_of(me * rows, rows), rows)
+    ]
+
+    each_target(finish)
     for d in order:
         each_piece(d, lambda piece: send_on(d, piece, finish))
         each_piece(d, lambda piece: send_turned(d, piece, finish))
-        each_piece(d, lambda piece: send_last(d, piece, finish))
-
-
-def gather_project(sequence, parts, count):
+
+    def finish_partial(pair, carry):
+        partial_copy(pair).wait_send()
+        return carry
+
+    lax.fori_loop(0, count // CORES, finish_partial, 0)
+
+    def finish_out(step, carry):
+        other = (me + step) % count
+        out_copy(other, other, other).wait()
+        return carry
+
+    lax.fori_loop(1, count, finish_out, 0)
+
+
+def gather_operate(sequence, parts, taps, skip, tables, count, groups):
     rows, features = sequence.shape
     own, depth = parts.shape[1:]
+    lanes = own // 3
     pieces = rows // PIECE
+    total = rows * count
+    inputs = (sequence, parts, taps, skip, *tables)
     return pl.pallas_call(
-        functools.partial(gather_kernel, count),
-        out_shape=jax.ShapeDtypeStruct((own, rows * count), jnp.bfloat16),
-        in_specs=[pl.BlockSpec(memory_space=pltpu.VMEM)] * 2,
+        functools.partial(gather_kernel, count, groups),
+        out_shape=jax.ShapeDtypeStruct((lanes * count, rows), jnp.bfloat16),
+        in_specs=[pl.BlockSpec(memory_space=pltpu.VMEM)] * len(inputs),
         out_specs=pl.BlockSpec(memory_space=pltpu.VMEM),
         scratch_shapes=[
-            pltpu.VMEM((2, count * rows, features), jnp.bfloat16),
+            pltpu.VMEM((total, features), jnp.bfloat16),
             pltpu.VMEM((2, own, features), jnp.bfloat16),
+            pltpu.VMEM((own, total), jnp.float32),
+            pltpu.VMEM((own, total), jnp.float32),
+            pltpu.VMEM((own, total), jnp.float32),
+            pltpu.VMEM((lanes, total), jnp.bfloat16),
+            pltpu.SemaphoreType.DMA((count,)),
+            pltpu.SemaphoreType.DMA((2, count // 2)),
+            pltpu.SemaphoreType.DMA((4, count, pieces)),
+            pltpu.SemaphoreType.DMA((count, pieces)),
+            pltpu.SemaphoreType.DMA((count // CORES,)),
+            pltpu.SemaphoreType.DMA((count // CORES,)),
             pltpu.SemaphoreType.DMA((count,)),
             pltpu.SemaphoreType.DMA((count,)),
-            pltpu.SemaphoreType.DMA((5, 2, count, pieces)),
-            pltpu.SemaphoreType.DMA((2, count, pieces)),
         ],
         compiler_params=pltpu.CompilerParams(
             collective_id=0, has_side_effects=True, vmem_limit_bytes=40 * 2**20
         ),
-        name="gather_project",
-    )(sequence, parts)
+        name="gather_operate",
+    )(*inputs)
 
 
 def filter_tables(decay_rates, residues):
@@ -466,14 +515,7 @@
     )
     taps = own_part(short_taps, own, 2).transpose(0, 2, 1)
     skip = own_part(skip_gain, own, 0)[:, None]
-    projections = gather_project(sequence, parts, count)
-    mixed = pl.pallas_call(
-        functools.partial(operator_kernel, groups),
-        out_shape=jax.ShapeDtypeStruct((own, total), jnp.bfloat16),
-        compiler_params=pltpu.CompilerParams(vmem_limit_bytes=32 * 2**20),
-        name="operator",
-    )(projections.reshape(slots, own, total), taps, skip, *tables)
-    mixed = lax.all_to_all(mixed, "ctx", split_axis=1, concat_axis=0, tiled=True)
+    mixed = gather_operate(sequence, parts, taps, skip, tables, count, groups)
     return mixed.T
 
 

time: 131 us -> 127 us (0.969); the launches traced: 131 us -> 125 us
  blocking collectives: 13.6 us -> 0 us
  Pallas kernels: 112 us -> 119 us
    all_to_all x1 -> x0, blocking collectives: 13.6 us -> none  [spread_channels(): lax.all_to_all(mixed, 'ctx', split_axis=1, concat_axis=0, tiled=True)]
    pallas_call x2 -> x1, Pallas kernels: 112 us -> 119 us  [gather_operate(): pl.pallas_call(functools.partial(gather_kernel, count, groups), out_shape...]
where the time goes in v3:
time: 127 us; the launch traced here: 125 us
  Pallas kernels  119 us (94%)
  local copies, waits for them, and re-layouts  4.1 us (3%)
  other arithmetic  1.32 us (1%)
    pallas_call x1, Pallas kernels, gather_operate(): pl.pallas_call(functools.partial(gather_kernel, count, groups), out_shape...  119 us

profile of v3, /device:TPU:0, one launch (start us, length us, event | category | flops | bytes accessed | tf_op | source)
XLA Modules:
  0.0 124.9 jit_solution(16646522338326068296)
XLA Ops:
  0.0 0.0 copy-start
  0.0 1.7 %copy.42 = bf16[3,256,1024]{1,2,0:T(8,128)(2,1)S(1)} copy(bf16[3,256,1024]{2,1,0:T(8,128)(2,1)} %param.7) | data formatting | bytes 3145728 | tf_op args[1]
  1.7 0.0 copy-start.2
  1.8 0.0 copy-start.3
  1.8 0.2 copy.43
  2.0 0.0 copy-done
  2.0 0.1 constant_dynamic-slice_fusion.2
  2.0 0.0 copy-start.1
  2.0 0.1 copy.50
  2.2 0.8 dynamic-slice_bitcast_fusion
  3.0 0.1 copy.47.skip_ref
  3.1 0.0 copy-done.2
  3.1 0.0 copy-done.3
  3.1 0.1 constant_dynamic-slice_fusion
  3.2 0.1 copy.52
  3.3 0.1 copy.51
  3.3 1.1 multiply_reduce_fusion
  4.5 0.1 multiply_exponential_fusion.into_ref
  4.6 0.1 exponential_multiply_fusion.out_of_ref
  4.7 0.0 copy-done.1
  4.7 119.3 %gather_operate.1 = bf16[1024,128]{1,0:T(8,128)(2,1)S(1)} custom-call(bf16[128,2048]{1,0:T(8,128)(2,1)S(1)} %copy-done.1, bf16[16,192,256]{2,1,0:T(8,128)(2,1)S(1)} %bitcast.11, f32[3,64,7]{2,1,0:T(8,128)S(1)} %bitcast.13, f32[64,1]{1,0:T(8,128)S(1)} %copy.47.skip_ref, f32[4,128,128]{2,1,0:T(8,128)S(1)} %broadcast_select_fusion.near_ref, ...), custom_call_target="tpu_custom_call" | custom-call | tf_op jit(solution)/shard_map/gather_operate/pallas_call | solution.py:455
  124.1 0.9 copy.49
  (6 shorter events, 0.1 us)
Async XLA Ops:
  0.0 2.0 %copy-start = (f32[3,7,1024]{2,1,0:T(8,128)S(1)}, f32[3,7,1024]{2,1,0:T(8,128)}, u32[]{:S(2)}) copy-start(f32[3,7,1024]{2,1,0:T(8,128)} %param.8) | copy-start | bytes 258052
  1.7 1.3 %copy-start.2 = (f32[64,16]{0,1:T(8,128)S(1)}, f32[64,16]{0,1:T(8,128)}, u32[]{:S(2)}) copy-start(f32[64,16]{0,1:T(8,128)} %param.9) | copy-start | bytes 12292
  1.8 1.3 %copy-start.3 = (f32[64,16]{0,1:T(8,128)S(1)}, f32[64,16]{0,1:T(8,128)}, u32[]{:S(2)}) copy-start(f32[64,16]{0,1:T(8,128)} %param.10) | copy-start | bytes 12292
  2.0 2.7 %copy-start.1 = (bf16[128,2048]{1,0:T(8,128)(2,1)S(1)}, bf16[128,2048]{1,0:T(8,128)(2,1)}, u32[]{:S(2)}) copy-start(bf16[128,2048]{1,0:T(8,128)(2,1)} %seq_ref.1) | copy-start | bytes 1572868
